TPU v7x, 32 devices: a whole 2x2x4 slice. The times are simulated.
32 devices in a mesh: groups: 2 (over y), dp: 4 (over z), section: 2 (over x), tensor: 2 (over core).
Axes of the slice: x: 2, y: 2, z: 4, core: 2. Of those that a mesh axis runs over, the one named last changes fastest.
Arguments:
- x_in: bfloat16 [4, 128, 8192], P('groups', None, ('dp', 'tensor')), parts along dimension 0, may hold values from -100 to 100
- subtree_end: int32 [4, 128], P('groups'), parts along dimension 0, may hold values from 0 to 127, as said below
- norm_gain: bfloat16 [2, 8192], P('section', ('dp', 'tensor')), may hold values from 0.5 to 1.5
- w_query: bfloat16 [2, 8192, 1024], P('section', None, ('dp', 'tensor')), may hold values from -1 to 1
- w_kv: bfloat16 [2, 8192, 256], P('section', None, ('dp', 'tensor')), may hold values from -20 to 20
- w_out: bfloat16 [2, 1024, 8192], P('section', None, ('dp', 'tensor')), may hold values from -0.1875 to 0.1875
- a_query: bfloat16 [2, 8192, 64], P('section'), may hold values from -0.0625 to 0.0625
- b_query: bfloat16 [2, 64, 1024], P('section', None, ('dp', 'tensor')), may hold values from -0.75 to 0.75
- a_out: bfloat16 [2, 1024, 64], P('section'), may hold values from -0.1875 to 0.1875
- b_out: bfloat16 [2, 64, 8192], P('section', None, ('dp', 'tensor')), may hold values from -0.75 to 0.75
- grad_a_query: float32 [2, 4, 8192, 64], P('section', 'dp'), may hold values from -0.03125 to 0.03125
- grad_b_query: float32 [2, 4, 64, 1024], P('section', 'dp'), may hold values from -0.5 to 0.5
- grad_a_out: float32 [2, 4, 1024, 64], P('section', 'dp'), may hold values from -0.09375 to 0.09375
- grad_b_out: float32 [2, 4, 64, 8192], P('section', 'dp'), may hold values from -0.5 to 0.5
Outputs:
- hidden_states: bfloat16 [2, 4, 128, 8192], P('section', 'groups', None, ('dp', 'tensor')), parts along dimension 1
There are 2 independent parts, one for each index of `groups`. A program takes and returns all parts, laid end to end along the dimension named above; an argument that names none is the same for every part. Nothing has to cross between parts.
Inputs may be any that keep to these rules, and one draw needn't show every extreme that they name: Tokens stand in depth-first order of one tree rooted at position 0; the descendants of token j are exactly positions j + 1 to subtree_end[m, j].
All inputs are finite; a program needn't handle non-finite values.
Results may differ from a plain program's by a relative error of at most 0.0077.
Values may be sent and summed in bfloat16 or wider, within the bound.
A program may use at most 64 MiB of HBM per device.

v0:
```python
import jax
import jax.numpy as jnp
from jax import lax
from jax.sharding import PartitionSpec as P

HD = 128
GROUP = 8


RATE = 0.5
EPS = 1e-05


def shifted(value, axis, steps):
    count = lax.axis_size(axis)
    leading, last = (max(0, -steps), min(count, count - steps))
    return lax.ppermute(value, axis, [(source, source + steps) for source in range(leading, last)])


def updated(factor, summed):
    return (factor.astype(jnp.float32) - RATE * summed).astype(jnp.bfloat16)


def on_device(
    x_in,
    subtree_end,
    norm_gain,
    w_query,
    w_kv,
    w_out,
    a_query,
    b_query,
    a_out,
    b_out,
    grad_a_query,
    grad_b_query,
    grad_a_out,
    grad_b_out,
):
    shard = lax.axis_index(("dp", "tensor"))
    head_cols = w_query.shape[2]
    feat_cols = w_out.shape[2]
    model_width = w_query.shape[1]
    micro = x_in.shape[0]
    tok = x_in.shape[1]
    part_aq = grad_a_query[0, 0]
    part_bq = grad_b_query[0, 0]
    part_ao = grad_a_out[0, 0]
    part_bo = grad_b_out[0, 0]
    sum_aq, sum_bq, sum_ao, sum_bo = lax.psum((part_aq, part_bq, part_ao, part_bo), "dp")
    sum_bq = lax.dynamic_slice_in_dim(sum_bq, shard * head_cols, head_cols, 1)
    sum_bo = lax.dynamic_slice_in_dim(sum_bo, shard * feat_cols, feat_cols, 1)
    new_aq = updated(a_query[0], sum_aq)
    new_ao = updated(a_out[0], sum_ao)
    new_bq = updated(b_query[0], sum_bq)
    new_bo = updated(b_out[0], sum_bo)
    merged_q = (
        w_query[0].astype(jnp.float32) + jnp.dot(new_aq, new_bq, preferred_element_type=jnp.float32)
    ).astype(jnp.bfloat16)
    merged_o = (
        w_out[0].astype(jnp.float32) + jnp.dot(new_ao, new_bo, preferred_element_type=jnp.float32)
    ).astype(jnp.bfloat16)
    w_proj = jnp.concatenate([merged_q, w_kv[0]], axis=1)
    heads_here = head_cols // HD
    group_index = shard * heads_here // GROUP
    section = lax.axis_index("section")
    n_section = lax.axis_size("section")
    ticks = micro + n_section - 1
    received = jnp.zeros((tok, feat_cols), jnp.bfloat16)
    results = jnp.zeros((micro, tok, feat_cols), jnp.bfloat16)
    for tick in range(ticks):
        index = tick - section
        valid = (index >= 0) & (index < micro)
        clipped = jnp.clip(index, 0, micro - 1)
        entering = lax.dynamic_index_in_dim(x_in, clipped, 0, keepdims=False)
        hidden = jnp.where(section == 0, entering, received)
        ends = lax.dynamic_index_in_dim(subtree_end, clipped, 0, keepdims=False)
        rows = lax.all_gather(hidden, ("dp", "tensor"), axis=1, tiled=True)
        gains = lax.all_gather(norm_gain, ("dp", "tensor"), axis=1, tiled=True)
        wide = rows.astype(jnp.float32)
        scaled = (wide * gains.astype(jnp.float32)).astype(jnp.bfloat16)
        acc = jnp.dot(scaled, w_proj, preferred_element_type=jnp.float32)
        layer_squares = jnp.sum(wide * wide, axis=1)
        inverse = lax.rsqrt(layer_squares / model_width + EPS)[:, None]
        query = (acc[:, :head_cols] * inverse).astype(jnp.bfloat16)
        kv_part = (acc[:, head_cols:] * inverse).astype(jnp.bfloat16)
        kv_all = lax.all_gather(kv_part, ("dp", "tensor"), axis=1, tiled=True)
        keys = lax.dynamic_slice_in_dim(kv_all, group_index * 2 * HD, HD, 1)
        values = lax.dynamic_slice_in_dim(kv_all, group_index * 2 * HD + HD, HD, 1)
        query = query.reshape(tok, heads_here, HD)
        scores = jnp.einsum(
            "qhd,kd->hqk", query, keys, preferred_element_type=jnp.float32
        ) * HD ** (-0.5)
        places = jnp.arange(tok)
        visible = (places[None, :] <= places[:, None]) & (ends[None, :] >= places[:, None])
        scores = jnp.where(visible[None], scores, -1e30)
        top = jnp.max(scores, axis=-1, keepdims=True)
        layer_weights = jnp.exp(scores - top)
        layer_weights = (layer_weights / jnp.sum(layer_weights, axis=-1, keepdims=True)).astype(
            jnp.bfloat16
        )
        mixed = jnp.einsum("hqk,kd->qhd", layer_weights, values, preferred_element_type=jnp.float32)
        mixed = mixed.astype(jnp.bfloat16).reshape(tok, head_cols)
        total = jnp.dot(
            lax.all_gather(mixed, ("dp", "tensor"), axis=1, tiled=True),
            merged_o,
            preferred_element_type=jnp.float32,
        )
        output = (hidden.astype(jnp.float32) + total).astype(jnp.bfloat16)
        stored = lax.dynamic_update_index_in_dim(results, output, clipped, 0)
        results = jnp.where(valid, stored, results)
        if tick + 1 < ticks:
            received = shifted(output, "section", 1)
    return results[None]


def solution(mesh):
    placed = (
        P("groups", None, ("dp", "tensor")),
        P("groups", None),
        P("section", ("dp", "tensor")),
        P("section", None, ("dp", "tensor")),
        P("section", None, ("dp", "tensor")),
        P("section", None, ("dp", "tensor")),
        P("section", None, None),
        P("section", None, ("dp", "tensor")),
        P("section", None, None),
        P("section", None, ("dp", "tensor")),
        P("section", "dp", None, None),
        P("section", "dp", None, None),
        P("section", "dp", None, None),
        P("section", "dp", None, None),
    )
    return jax.shard_map(
        on_device,
        mesh=mesh,
        in_specs=placed,
        out_specs=P("section", "groups", None, ("dp", "tensor")),
        check_vma=False,
    )
```

profile of v0, /device:TPU:3, one launch (start us, length us, event | category | flops | bytes accessed | tf_op | source)
XLA Modules:
  0.0 389.2 jit_solution(12061405842557746687)
XLA Ops:
  7.4 1.7 dynamic-slice_select_fusion
  9.1 0.5 all-reduce.3.cloned.1.call-update
  9.8 2.9 copy.15
  12.7 14.9 %all_gather.33 = bf16[1,8192]{1,0:T(2,128)(2,1)S(1)} all-gather(bf16[1,1024]{1,0:T(2,128)(2,1)S(1)} %copy-done.14), channel_id=1, replica_groups=mesh['groups'=2,'dp'=4,'section'=2,'tensor'=2] {'dp','tensor'}, dimensions={1}, use_global_device_ids=true | all-gather | bytes 18432 | tf_op jit(solution)/shard_map/all_gather | solution.py:79
  27.7 89.0 %all-gather.12.cloned.1.call-done = bf16[1,128,8192]{2,1,0:T(8,128)(2,1)} async-done(((bf16[1,128,1024]{2,1,0:T(8,128)(2,1)}), bf16[1,128,8192]{2,1,0:T(8,128)(2,1)}) %all-gather.12.cloned.1.call-update) | async-done | bytes 2097168 | tf_op jit(solution)/shard_map/all_gather | solution.py:78
  116.7 2.3 fusion.6
  119.0 79.4 %all-reduce.3.cloned.1.call-done = (f32[1024,64]{0,1:T(8,128)}, f32[64,8192]{1,0:T(8,128)}, f32[8192,64]{0,1:T(8,128)}, f32[64,1024]{1,0:T(8,128)}) async-done(((f32[1024,64]{0,1:T(8,128)}, f32[64,8192]{1,0:T(8,128)}, f32[8192,64]{0,1:T(8,128)}, f32[64,1024]{1,0:T(8,128)}), (f32[1024,64]{0,1:T(8,128)}, f32[64,8192]{1,0:T(8,128)}, f32[8192,64]{0,1:T(8,128)}, ...) | async-done | bytes 4718608 | tf_op jit(solution)/shard_map/psum | solution.py:50
  198.4 2.6 fusion
  201.0 0.9 fusion.8
  202.3 14.7 %all_gather.34 = bf16[128,256]{0,1:T(8,128)(2,1)S(1)} all-gather(bf16[128,32]{0,1:T(8,128)(2,1)S(1)} %fusion.85), channel_id=1, replica_groups=mesh['groups'=2,'dp'=4,'section'=2,'tensor'=2] {'dp','tensor'}, dimensions={1}, use_global_device_ids=true | all-gather | bytes 73728 | tf_op jit(solution)/shard_map/all_gather | solution.py:87
  217.4 14.2 %all-gather.1 = bf16[128,1,1024]{0,2,1:T(8,128)(2,1)S(1)} all-gather(bf16[128,1,128]{0,2,1:T(8,128)(2,1)S(1)} %fusion.26), channel_id=3, replica_groups=mesh['groups'=2,'dp'=4,'section'=2,'tensor'=2] {'dp','tensor'}, dimensions={2}, use_global_device_ids=true | all-gather | bytes 294912 | tf_op jit(solution)/shard_map/all_gather | solution.py:105
  231.7 1.7 fusion.7
  233.5 0.5 bitcast_dynamic-update-slice_fusion
  234.0 1.3 collective-permute-start
  235.3 8.3 %collective-permute-done = bf16[128,1024]{1,0:T(8,128)(2,1)S(1)} collective-permute-done((bf16[128,1024]{1,0:T(8,128)(2,1)S(1)}, bf16[128,1024]{1,0:T(8,128)(2,1)S(1)}, u32[]{:S(2)}, u32[]{:S(2)}) %collective-permute-start) | collective-permute-done | bytes 262176 | tf_op jit(solution)/shard_map/ppermute | solution.py:17
  243.6 0.7 bitcast_select_fusion.2
  244.4 28.8 %all-gather.8.cloned.1.call-done = bf16[128,8192]{1,0:T(8,128)(2,1)} async-done(((bf16[128,1024]{1,0:T(8,128)(2,1)}), bf16[128,8192]{1,0:T(8,128)(2,1)}) %all-gather.8.cloned.1.call-update) | async-done | bytes 2097168 | tf_op jit(solution)/shard_map/all_gather | solution.py:78
  273.2 2.2 fusion.2
  275.5 2.7 fusion.12
  278.2 14.1 %all_gather.37 = bf16[128,256]{0,1:T(8,128)(2,1)S(1)} all-gather(bf16[128,32]{0,1:T(8,128)(2,1)S(1)} %fusion.84), channel_id=1, replica_groups=mesh['groups'=2,'dp'=4,'section'=2,'tensor'=2] {'dp','tensor'}, dimensions={1}, use_global_device_ids=true | all-gather | bytes 73728 | tf_op jit(solution)/shard_map/all_gather | solution.py:87
  292.6 14.2 %all-gather.2 = bf16[128,1,1024]{0,2,1:T(8,128)(2,1)S(1)} all-gather(bf16[128,1,128]{0,2,1:T(8,128)(2,1)S(1)} %fusion.27), channel_id=4, replica_groups=mesh['groups'=2,'dp'=4,'section'=2,'tensor'=2] {'dp','tensor'}, dimensions={2}, use_global_device_ids=true | all-gather | bytes 294912 | tf_op jit(solution)/shard_map/all_gather | solution.py:105
  306.9 0.5 fusion.42
  307.4 1.3 collective-permute-start.1
  308.7 8.3 %collective-permute-done.1 = bf16[128,1024]{1,0:T(8,128)(2,1)S(1)} collective-permute-done((bf16[128,1024]{1,0:T(8,128)(2,1)S(1)}, bf16[128,1024]{1,0:T(8,128)(2,1)S(1)}, u32[]{:S(2)}, u32[]{:S(2)}) %collective-permute-start.1) | collective-permute-done | bytes 262176 | tf_op jit(solution)/shard_map/ppermute | solution.py:17
  317.0 0.7 bitcast_select_fusion
  317.8 0.8 copy.22
  318.6 28.7 %all-gather.10.cloned.1.call-done = bf16[128,8192]{1,0:T(8,128)(2,1)} async-done(((bf16[128,1024]{1,0:T(8,128)(2,1)}), bf16[128,8192]{1,0:T(8,128)(2,1)}) %all-gather.10.cloned.1.call-update) | async-done | bytes 2097168 | tf_op jit(solution)/shard_map/all_gather | solution.py:78
  347.2 2.2 fusion.4
  349.5 2.6 fusion.10
  352.2 14.1 %all_gather.40 = bf16[128,256]{0,1:T(8,128)(2,1)S(1)} all-gather(bf16[128,32]{0,1:T(8,128)(2,1)S(1)} %fusion.83), channel_id=1, replica_groups=mesh['groups'=2,'dp'=4,'section'=2,'tensor'=2] {'dp','tensor'}, dimensions={1}, use_global_device_ids=true | all-gather | bytes 73728 | tf_op jit(solution)/shard_map/all_gather | solution.py:87
  366.6 14.2 %all-gather.3 = bf16[128,1,1024]{0,2,1:T(8,128)(2,1)S(1)} all-gather(bf16[128,1,128]{0,2,1:T(8,128)(2,1)S(1)} %fusion.28), channel_id=5, replica_groups=mesh['groups'=2,'dp'=4,'section'=2,'tensor'=2] {'dp','tensor'}, dimensions={2}, use_global_device_ids=true | all-gather | bytes 294912 | tf_op jit(solution)/shard_map/all_gather | solution.py:105
  380.9 1.2 fusion.35
  (59 shorter events, 2.0 us)
Async XLA Ops:
  7.4 109.4 %all-gather.12.cloned.1.call-start = ((), (), s32[]{:S(2)}) async-start(), calls=%async_computation.2 | async-start | bytes 2359296 | tf_op jit(solution)/shard_map/all_gather | solution.py:78
  9.1 189.3 %all-reduce.3.cloned.1.call-start = ((), (), s32[]{:S(2)}) async-start(), calls=%async_computation.3 | async-start | bytes 9437184 | tf_op jit(solution)/shard_map/psum | solution.py:50
  9.6 263.6 %all-gather.8.cloned.1.call-start = ((), (), s32[]{:S(2)}) async-start(), calls=%async_computation | async-start | bytes 2359296 | tf_op jit(solution)/shard_map/all_gather | solution.py:78
  9.7 2.9 copy-start.14
  9.7 17.9 %copy-start.15 = (s32[2,128]{1,0:T(2,128)S(1)}, s32[2,128]{1,0:T(2,128)}, u32[]{:S(2)}) copy-start(s32[2,128]{1,0:T(2,128)} %param.15) | copy-start | bytes 3076
  12.7 185.7 %copy-start.9 = (bf16[1,8192,64]{1,2,0:T(8,128)(2,1)S(1)}, bf16[1,8192,64]{1,2,0:T(8,128)(2,1)}, u32[]{:S(2)}) copy-start(bf16[1,8192,64]{1,2,0:T(8,128)(2,1)} %param.20) | copy-start | bytes 3145732
  12.7 185.7 %copy-start.13 = (bf16[1,64,128]{2,1,0:T(8,128)(2,1)S(1)}, bf16[1,64,128]{2,1,0:T(8,128)(2,1)}, u32[]{:S(2)}) copy-start(bf16[1,64,128]{2,1,0:T(8,128)(2,1)} %param.21) | copy-start | bytes 49156
  198.4 2.6 copy-start.3
  198.4 2.6 copy-start.16
  200.9 1.3 copy-start.7
  201.0 30.7 %copy-start.6 = (bf16[1,1024,1024]{2,1,0:T(8,128)(2,1)S(1)}, bf16[1,1024,1024]{2,1,0:T(8,128)(2,1)}, u32[]{:S(2)}) copy-start(bf16[1,1024,1024]{2,1,0:T(8,128)(2,1)} %param.19) | copy-start | bytes 6291460
  201.0 30.6 %copy-start.10 = (f32[1024,64]{0,1:T(8,128)S(1)}, f32[1024,64]{0,1:T(8,128)}, u32[]{:S(2)}) copy-start(f32[1024,64]{0,1:T(8,128)} %get-tuple-element.5) | copy-start | bytes 786436
  201.0 30.6 %copy-start.11 = (bf16[1,64,1024]{2,1,0:T(8,128)(2,1)S(1)}, bf16[1,64,1024]{2,1,0:T(8,128)(2,1)}, u32[]{:S(2)}) copy-start(bf16[1,64,1024]{2,1,0:T(8,128)(2,1)} %param.23) | copy-start | bytes 393220
  201.0 30.6 %copy-start.12 = (bf16[1,1024,64]{1,2,0:T(8,128)(2,1)S(1)}, bf16[1,1024,64]{1,2,0:T(8,128)(2,1)}, u32[]{:S(2)}) copy-start(bf16[1,1024,64]{1,2,0:T(8,128)(2,1)} %param.22) | copy-start | bytes 393220
  231.6 1.8 copy-start
  233.4 10.2 %copy-start.8 = (bf16[2,128,1024]{2,1,0:T(8,128)(2,1)S(1)}, bf16[2,128,1024]{2,1,0:T(8,128)(2,1)}, u32[]{:S(2)}) copy-start(bf16[2,128,1024]{2,1,0:T(8,128)(2,1)} %param.14) | copy-start | bytes 1572868
  234.0 9.6 %collective-permute-start = (bf16[128,1024]{1,0:T(8,128)(2,1)S(1)}, bf16[128,1024]{1,0:T(8,128)(2,1)S(1)}, u32[]{:S(2)}, u32[]{:S(2)}) collective-permute-start(bf16[128,1024]{1,0:T(8,128)(2,1)S(1)} %get-tuple-element.15), channel_id=1, source_target_pairs={{0,2},{1,3},{4,6},{5,7},{8,10},{9,11},{12,14},{13,15},{16,18},{17,... | collective-permute-start | bytes 786440 | tf_op jit(solution)/shard_map/ppermute | solution.py:17
  244.4 102.8 %all-gather.10.cloned.1.call-start = ((), (), s32[]{:S(2)}) async-start(), calls=%async_computation.1 | async-start | bytes 2359296 | tf_op jit(solution)/shard_map/all_gather | solution.py:78
  273.2 2.2 copy-start.5
  275.5 31.4 %copy-start.2 = (bf16[128,1024]{1,0:T(8,128)(2,1)S(1)}, bf16[128,1024]{1,0:T(8,128)(2,1)}, u32[]{:S(2)}) copy-start(bf16[128,1024]{1,0:T(8,128)(2,1)} %bitcast_select_fusion.2) | copy-start | bytes 786436
  307.4 9.6 %collective-permute-start.1 = (bf16[128,1024]{1,0:T(8,128)(2,1)S(1)}, bf16[128,1024]{1,0:T(8,128)(2,1)S(1)}, u32[]{:S(2)}, u32[]{:S(2)}) collective-permute-start(bf16[128,1024]{1,0:T(8,128)(2,1)S(1)} %get-tuple-element.19), channel_id=1, source_target_pairs={{0,2},{1,3},{4,6},{5,7},{8,10},{9,11},{12,14},{13,15},{16,18},{17,... | collective-permute-start | bytes 786440 | tf_op jit(solution)/shard_map/ppermute | solution.py:17
  347.2 2.2 copy-start.4
  349.5 31.4 %copy-start.1 = (bf16[128,1024]{1,0:T(8,128)(2,1)S(1)}, bf16[128,1024]{1,0:T(8,128)(2,1)}, u32[]{:S(2)}) copy-start(bf16[128,1024]{1,0:T(8,128)(2,1)} %bitcast_select_fusion) | copy-start | bytes 786436
Sparse Core Ops, SparseCore 0:
  9.8 106.8 all-gather.11
  244.5 28.6 all-gather.7
  317.9 29.3 all-gather.9
Sparse Core Ops, SparseCore 1:
  12.1 186.1 all-reduce.2
where the time goes:
time: 391 us; the launch traced here: 389 us
  waiting for transfers between devices  243 us (62%)
  blocking collectives  100 us (26%)
  between operations  14.9 us (4%)
  matrix products  13.7 us (4%)
  other arithmetic  10.1 us (3%)
  local copies, waits for them, and re-layouts  4.26 us (1%)
    all_gather x3, waiting for transfers between devices, on_device(): rows = lax.all_gather(hidden, ('dp', 'tensor'), axis=1, tiled=True)  146 us
    psum x1, waiting for transfers between devices, on_device(): lax.psum((part_aq, part_bq, part_ao, part_bo), 'dp')  79.4 us
    all_gather x3, blocking collectives, on_device(): kv_all = lax.all_gather(kv_part, ('dp', 'tensor'), axis=1, tiled=True)  42.8 us
    all_gather x3, blocking collectives, on_device(): lax.all_gather(mixed, ('dp', 'tensor'), axis=1, tiled=True)  42.7 us
    ppermute x2, waiting for transfers between devices, shifted(): lax.ppermute(value, axis, [(source, source + steps) for source in range(l...  16.7 us
    all_gather x1, blocking collectives, on_device(): gains = lax.all_gather(norm_gain, ('dp', 'tensor'), axis=1, tiled=True)  14.9 us
  transfers between devices with their start and end apart: 6, of which 6 were waited for; matrix products, arithmetic and copies ran while one was open for 2% of the time, Pallas kernels for 0%

commit v1 on v0

v1 whole, which is shorter than its diff:
```python
import functools

import jax
import jax.numpy as jnp
from jax import lax
from jax.experimental import pallas as pl
from jax.experimental.pallas import tpu as pltpu
from jax.sharding import PartitionSpec as P

HD = 128
GROUP = 8
RATE = 0.5
EPS = 1e-05
MESH = pl.DeviceIdType.MESH
F32 = jnp.float32
BF16 = jnp.bfloat16


def chain(
    sizes,
    x_ref,
    ends_ref,
    gain_ref,
    g_ref,
    base_ref,
    wq_hbm,
    wx_hbm,
    wo_hbm,
    out_ref,
    wcat,
    merged,
    blocks,
    squares,
    hidden,
    kvx,
    mix,
    grecv,
    aot,
    bo,
    bpad,
    acc,
    scaled_q,
    w_sem,
    blk_send,
    blk_fwd,
    blk_recv,
    sq_send,
    sq_recv,
    kv_send,
    kv_recv,
    mix_send,
    mix_recv,
    g_send,
    g_recv,
    ao_send,
    ao_recv,
    hid_send,
    hid_recv,
):
    n_dp, n_section, kv_cols = sizes
    n = 2 * n_dp
    micro, tok, feat = x_ref.shape
    rank = base_ref.shape[0]
    width = n * feat
    d, t, s = lax.axis_index("dp"), lax.axis_index("tensor"), lax.axis_index("section")
    me = 2 * d + t

    def peer(k):
        return lax.rem(me + k, n)

    def place(i):
        return {"dp": i // 2, "tensor": lax.rem(i, 2)}

    def along(k):
        return lax.rem(d + k, n_dp)

    def loop(low, high, body):
        def step(k, carry):
            body(k)
            return carry

        lax.fori_loop(low, high, step, jnp.int32(0))

    def weights(k):
        if k == 0:
            return pltpu.make_async_copy(wq_hbm, wcat.at[:, pl.ds(0, HD)], w_sem.at[0])
        if k == 1:
            return pltpu.make_async_copy(wx_hbm, wcat.at[:, pl.ds(HD, HD)], w_sem.at[1])
        return pltpu.make_async_copy(wo_hbm, merged, w_sem.at[2])

    def block_copy(m, i, send, to):
        return pltpu.make_async_remote_copy(
            src_ref=blocks.at[m, i],
            dst_ref=blocks.at[m, i],
            send_sem=send,
            recv_sem=blk_recv.at[m, i],
            device_id=to,
            device_id_type=MESH,
        )

    def to_shard(m, k):
        return block_copy(m, me, blk_send.at[m, k], {"dp": along(k), "tensor": t})

    def to_sibling(m):
        return block_copy(m, me, blk_send.at[m, 0], {"tensor": 1 - t})

    def forward(m, k):
        return block_copy(m, 2 * along(k) + t, blk_fwd.at[m, k], {"tensor": 1 - t})

    def spread(buffer, send, recv, k, i):
        return pltpu.make_async_remote_copy(
            src_ref=buffer.at[i],
            dst_ref=buffer.at[i],
            send_sem=send.at[k],
            recv_sem=recv.at[i],
            device_id=place(peer(k)),
            device_id_type=MESH,
        )

    small = (
        lambda m: (squares.at[m], sq_send.at[m], sq_recv.at[m]),
        lambda m: (kvx.at[m], kv_send.at[m], kv_recv.at[m]),
        lambda m: (mix.at[m], mix_send.at[m], mix_recv.at[m]),
        lambda m: (aot, ao_send, ao_recv),
    )

    def start_all(kind, m):
        loop(1, n, lambda k: spread(*small[kind](m), k, me).start())

    def arrive_all(kind, m):
        loop(1, n, lambda k: spread(*small[kind](m), k, peer(k)).wait_recv())

    def sent_all(kind, m):
        loop(1, n, lambda k: spread(*small[kind](m), k, me).wait_send())

    def grads(k):
        return pltpu.make_async_remote_copy(
            src_ref=g_ref.at[2 * along(k) + t],
            dst_ref=grecv.at[d],
            send_sem=g_send.at[k],
            recv_sem=g_recv.at[d],
            device_id={"dp": along(k), "tensor": t},
            device_id_type=MESH,
        )

    def grads_in(k):
        return pltpu.make_async_remote_copy(
            src_ref=g_ref.at[me],
            dst_ref=grecv.at[along(k)],
            send_sem=g_send.at[k],
            recv_sem=g_recv.at[along(k)],
            device_id={"dp": along(k), "tensor": t},
            device_id_type=MESH,
        )

    def onward(m, to):
        return pltpu.make_async_remote_copy(
            src_ref=out_ref.at[m],
            dst_ref=hidden.at[m],
            send_sem=hid_send.at[m],
            recv_sem=hid_recv.at[m],
            device_id={"section": to},
            device_id_type=MESH,
        )

    def enter(m):
        wide = hidden[m].astype(F32)
        blocks[m, me] = (wide * gain_ref[...]).astype(BF16)
        to_sibling(m).start()
        loop(1, n_dp, lambda k: to_shard(m, k).start())
        column = jnp.sum(wide * wide, axis=1, keepdims=True)
        squares[m, me] = jnp.transpose(jnp.broadcast_to(column, (tok, HD)))[:8]
        start_all(0, m)

    def enter_first(m):
        hidden[m] = x_ref[m]
        enter(m)

    def enter_later(m):
        onward(m, jnp.maximum(s - 1, 0)).wait_recv()
        enter(m)

    def project_block(m, i):
        rows = pl.ds(pl.multiple_of(i * feat, feat), feat)
        acc[...] += jnp.dot(blocks[m, i], wcat[rows, :], preferred_element_type=F32)

    def project(m):
        if m == 0:
            weights(0).wait()
            weights(1).wait()
        acc[...] = jnp.zeros_like(acc)
        project_block(m, me)

        def near(k):
            i = 2 * along(k) + t
            block_copy(m, i, blk_send.at[m, k], {"tensor": 1 - t}).wait_recv()
            forward(m, k).start()
            project_block(m, i)

        def far(k):
            i = 2 * along(k) + 1 - t
            block_copy(m, i, blk_send.at[m, k], {"tensor": 1 - t}).wait_recv()
            project_block(m, i)

        loop(1, n_dp, near)
        loop(0, n_dp, far)
        arrive_all(0, m)
        total = jnp.sum(squares[m], axis=0)[:1]
        column = jnp.transpose(jnp.broadcast_to(total, (tok, HD)))
        inverse = lax.rsqrt(column / width + EPS)
        scaled_q[...] = acc[:, :HD] * inverse
        kvx[m, me] = (acc[:, HD:] * inverse).astype(BF16)
        start_all(1, m)

    def update():
        total = g_ref[me].astype(F32)
        loop(1, n_dp, lambda k: grads_in(k).wait_recv())
        for k in range(1, n_dp):
            total = total + grecv[along(k)].astype(F32)
        fresh = (base_ref[...].astype(F32) - RATE * total).astype(BF16)
        bo[...] = fresh[:, :feat]
        bpad[...] = jnp.zeros_like(bpad)
        bpad[pl.ds(kv_cols, rank), :] = fresh[:, feat : feat + HD]
        aot[me] = fresh[:, feat + HD :]
        start_all(3, 0)

    def merge():
        weights(2).wait()
        arrive_all(3, 0)

        def rows_of(j):
            rows = pl.ds(pl.multiple_of(j * HD, HD), HD)
            product = lax.dot_general(
                aot[j], bo[...], (((0,), (0,)), ((), ())), preferred_element_type=F32
            )
            merged[rows, :] = (merged[rows, :].astype(F32) + product).astype(BF16)

        loop(0, n, rows_of)

    def attend(m):
        arrive_all(1, m)
        query = scaled_q[...]
        for k in range(n_dp):
            query = query + jnp.dot(kvx[m, 2 * k + t], bpad[...], preferred_element_type=F32)
        query = query.astype(BF16)
        per = HD // kv_cols
        first = me // GROUP * 2 * per
        spot = lax.broadcasted_iota(jnp.int32, (HD, HD), 0)
        lane = lax.broadcasted_iota(jnp.int32, (HD, HD), 1)
        keys = jnp.zeros((tok, HD), F32)
        values = jnp.zeros((tok, HD), F32)
        for i in range(per):
            pick = jnp.where((spot < kv_cols) & (lane == spot + i * kv_cols), 1.0, 0.0).astype(BF16)
            keys = keys + jnp.dot(kvx[m, first + i], pick, preferred_element_type=F32)
            values = values + jnp.dot(kvx[m, first + per + i], pick, preferred_element_type=F32)
        scores = lax.dot_general(
            query, keys.astype(BF16), (((1,), (1,)), ((), ())), preferred_element_type=F32
        ) * HD ** (-0.5)
        here = lax.broadcasted_iota(jnp.int32, (tok, tok), 0)
        there = lax.broadcasted_iota(jnp.int32, (tok, tok), 1)
        visible = (there <= here) & (ends_ref[m] >= here)
        scores = jnp.where(visible, scores, -1e30)
        raised = jnp.exp(scores - jnp.max(scores, axis=-1, keepdims=True))
        portion = (raised / jnp.sum(raised, axis=-1, keepdims=True)).astype(BF16)
        mixed = jnp.dot(portion, values.astype(BF16), preferred_element_type=F32)
        mix[m, me] = mixed.astype(BF16)
        start_all(2, m)

    def leave(m):
        arrive_all(2, m)
        heads = jnp.concatenate([mix[m, j] for j in range(n)], axis=1)
        total = jnp.dot(heads, merged[...], preferred_element_type=F32)
        out_ref[m] = (hidden[m].astype(F32) + total).astype(BF16)

        @pl.when(s < n_section - 1)
        def _():
            onward(m, jnp.minimum(s + 1, n_section - 1)).start()

    for k in range(3):
        weights(k).start()
    barrier = pltpu.get_barrier_semaphore()

    def greet(k):
        pl.semaphore_signal(barrier, inc=1, device_id=place(peer(k)), device_id_type=MESH)

    loop(1, n, greet)

    @pl.when(s > 0)
    def _():
        pl.semaphore_signal(barrier, inc=1, device_id={"section": s - 1}, device_id_type=MESH)

    @pl.when(s < n_section - 1)
    def _():
        pl.semaphore_signal(barrier, inc=1, device_id={"section": s + 1}, device_id_type=MESH)

    sections = (s > 0).astype(jnp.int32) + (s < n_section - 1).astype(jnp.int32)
    pl.semaphore_wait(barrier, n - 1 + sections)

    @pl.when(s == 0)
    def _():
        enter_first(0)

    loop(1, n_dp, lambda k: grads(k).start())

    @pl.when(s == 0)
    def _():
        for m in range(1, micro):
            enter_first(m)

    @pl.when(s > 0)
    def _():
        update()
        merge()
        enter_later(0)

    for m in range(micro):
        project(m)
        if m == 0:

            @pl.when(s == 0)
            def _():
                update()

        if m + 1 < micro:

            @pl.when(s > 0)
            def _(m=m):
                enter_later(m + 1)

        attend(m)
        if m == 0:

            @pl.when(s == 0)
            def _():
                merge()

        leave(m)

    loop(1, n_dp, lambda k: grads(k).wait_send())
    sent_all(3, 0)
    for m in range(micro):
        to_sibling(m).wait_send()
        loop(1, n_dp, lambda k: to_shard(m, k).wait_send())
        loop(1, n_dp, lambda k: forward(m, k).wait_send())
        for kind in range(3):
            sent_all(kind, m)

        @pl.when(s < n_section - 1)
        def _():
            onward(m, jnp.minimum(s + 1, n_section - 1)).wait_send()


def on_device(
    x_in,
    subtree_end,
    norm_gain,
    w_query,
    w_kv,
    w_out,
    a_query,
    b_query,
    a_out,
    b_out,
    grad_a_query,
    grad_b_query,
    grad_a_out,
    grad_b_out,
):
    n_dp, n_section = lax.axis_size("dp"), lax.axis_size("section")
    n = 2 * n_dp
    shard = lax.axis_index(("dp", "tensor"))
    micro, tok, feat = x_in.shape
    width, kv_cols = w_kv.shape[1:]
    rank = a_query.shape[2]
    own = (a_query[0].astype(F32) / n_dp - RATE * grad_a_query[0, 0]).astype(BF16)
    rest = jnp.zeros((width, HD - kv_cols - rank), BF16)
    w_side = jnp.concatenate([w_kv[0], own, rest], axis=1)
    sliced = [
        grad_b_out[0, 0].astype(BF16).reshape(rank, n, feat),
        grad_b_query[0, 0].astype(BF16).reshape(rank, n, HD),
        grad_a_out[0, 0].astype(BF16).T.reshape(rank, n, HD),
    ]
    gradients = jnp.concatenate(sliced, axis=2).transpose(1, 0, 2)
    rows = lax.dynamic_slice_in_dim(a_out[0], shard * HD, HD, 0)
    base = jnp.concatenate([b_out[0], b_query[0], rows.T], axis=1)
    vmem = pl.BlockSpec(memory_space=pltpu.VMEM)
    hbm = pl.BlockSpec(memory_space=pl.ANY)
    dma = pltpu.SemaphoreType.DMA
    extra = feat + 2 * HD
    return pl.pallas_call(
        functools.partial(chain, (n_dp, n_section, kv_cols)),
        out_shape=jax.ShapeDtypeStruct((micro, tok, feat), BF16),
        in_specs=[vmem] * 5 + [hbm] * 3,
        out_specs=vmem,
        scratch_shapes=[
            pltpu.VMEM((width, 2 * HD), BF16),
            pltpu.VMEM((n * HD, feat), BF16),
            pltpu.VMEM((micro, n, tok, feat), BF16),
            pltpu.VMEM((micro, n, 8, HD), F32),
            pltpu.VMEM((micro, tok, feat), BF16),
            pltpu.VMEM((micro, n, tok, HD), BF16),
            pltpu.VMEM((micro, n, tok, HD), BF16),
            pltpu.VMEM((n_dp, rank, extra), BF16),
            pltpu.VMEM((n, rank, HD), BF16),
            pltpu.VMEM((rank, feat), BF16),
            pltpu.VMEM((HD, HD), BF16),
            pltpu.VMEM((tok, 2 * HD), F32),
            pltpu.VMEM((tok, HD), F32),
            dma((3,)),
            dma((micro, n_dp)),
            dma((micro, n_dp)),
            dma((micro, n)),
            dma((micro, n)),
            dma((micro, n)),
            dma((micro, n)),
            dma((micro, n)),
            dma((micro, n)),
            dma((micro, n)),
            dma((n_dp,)),
            dma((n_dp,)),
            dma((n,)),
            dma((n,)),
            dma((micro,)),
            dma((micro,)),
        ],
        compiler_params=pltpu.CompilerParams(
            collective_id=0, has_side_effects=True, vmem_limit_bytes=48 * 2**20
        ),
    )(
        x_in,
        subtree_end[:, None, :],
        norm_gain.astype(F32),
        gradients,
        base,
        w_query[0],
        w_side,
        w_out[0],
    )[None]


def solution(mesh):
    placed = (
        P("groups", None, ("dp", "tensor")),
        P("groups", None),
        P("section", ("dp", "tensor")),
        P("section", None, ("dp", "tensor")),
        P("section", None, ("dp", "tensor")),
        P("section", None, ("dp", "tensor")),
        P("section", None, None),
        P("section", None, ("dp", "tensor")),
        P("section", None, None),
        P("section", None, ("dp", "tensor")),
        P("section", "dp", None, None),
        P("section", "dp", None, None),
        P("section", "dp", None, None),
        P("section", "dp", None, None),
    )
    return jax.shard_map(
        on_device,
        mesh=mesh,
        in_specs=placed,
        out_specs=P("section", "groups", None, ("dp", "tensor")),
        check_vma=False,
    )
```

time: 391 us -> 191 us (0.49)
  waiting for transfers between devices: 243 us -> 0 us
  Pallas kernels: 0 us -> 170 us
  blocking collectives: 100 us -> 0 us
  between operations: 14.9 us -> 0.18 us
  matrix products: 13.7 us -> 0 us
  local copies, waits for them, and re-layouts: 4.26 us -> 10.4 us
    pallas_call x0 -> x1, Pallas kernels: none -> 170 us  [on_device(): pl.pallas_call(functools.partial(chain, (n_dp, n_section, kv_cols)), out_...]
    all_gather x3 -> x0, waiting for transfers between devices: 146 us -> none  [on_device(): rows = lax.all_gather(hidden, ('dp', 'tensor'), axis=1, tiled=True)]
    all_gather x7 -> x0, blocking collectives: 100 us -> none  [the longest x3 42.8 us: on_device(): kv_all = lax.all_gather(kv_part, ('dp', 'tensor'), axis=1, tiled=True)]
    psum x1 -> x0, waiting for transfers between devices: 79.4 us -> none  [on_device(): lax.psum((part_aq, part_bq, part_ao, part_bo), 'dp')]
    ppermute x2 -> x0, waiting for transfers between devices: 16.7 us -> none  [shifted(): lax.ppermute(value, axis, [(source, source + steps) for source in range(l...]
    dot_general x14 -> x0, matrix products: 13.7 us -> none  [the longest x3 6.15 us: on_device(): acc = jnp.dot(scaled, w_proj, preferred_element_type=jnp.float32)]
    reduce_sum x6 -> x0, other arithmetic: 6.84 us -> none  [the longest x3 6.71 us: on_device(): layer_squares = jnp.sum(wide * wide, axis=1)]
    unnamed x36 -> x26, local copies, waits for them, and re-layouts: 4.2 us -> 9.72 us
  transfers between devices with their start and end apart: 6 -> 0, of which waited for: 6 -> 0; matrix products, arithmetic and copies ran while one was open for 2% -> 0% of each run, Pallas kernels for 0% -> 0%
where the time goes in v1:
time: 191 us
  Pallas kernels  170 us (89%)
  local copies, waits for them, and re-layouts  10.4 us (5%)
  other arithmetic  9.81 us (5%)
    pallas_call x1, Pallas kernels, on_device(): pl.pallas_call(functools.partial(chain, (n_dp, n_section, kv_cols)), out_...  170 us
    unnamed x26, local copies, waits for them, and re-layouts  9.72 us
    concatenate x1, other arithmetic, on_device(): w_side = jnp.concatenate([w_kv[0], own, rest], axis=1)  4.36 us
    convert_element_type x1, other arithmetic, on_device(): (a_query[0].astype(F32) / n_dp - RATE * grad_a_query[0, 0]).astype(BF16)  4.24 us

profile of v1, /device:TPU:3, one launch (start us, length us, event | category | flops | bytes accessed | tf_op | source)
XLA Modules:
  0.0 190.7 jit_solution(7993526604638735256)
XLA Ops:
  0.0 0.0 copy-start
  0.0 0.9 copy-done
  0.9 0.9 pad_maximum_fusion.base_ref
  1.9 0.0 copy-start.5
  1.9 3.9 %copy.23 = f32[1,1,8192,64]{3,2,1,0:T(8,128)} copy(f32[1,1,8192,64]{2,3,1,0:T(8,128)} %param.24) | data formatting | bytes 4194304 | tf_op args[10]
  5.7 0.0 copy-done.5
  5.7 1.1 copy.22
  6.8 0.0 copy-start.6
  6.8 4.2 %fusion = bf16[8192,64]{1,0:T(8,128)(2,1)} fusion(f32[1,1,8192,64]{3,2,1,0:T(8,128)} %copy.23, bf16[1,8192,64]{2,1,0:T(8,128)(2,1)S(1)} %copy.22), kind=kLoop, calls=%fused_computation.1 | loop fusion | flops 2621440 | bytes 4194304 | tf_op jit(solution)/shard_map/convert_element_type | solution.py:375
  11.1 0.0 copy-done.6
  11.1 1.0 copy.21
  12.1 0.1 pad.2.clone
  12.2 4.4 %maximum_maximum_fusion.wx_hbm = bf16[8192,128]{1,0:T(8,128)(2,1)} fusion(bf16[8192,64]{1,0:T(8,128)(2,1)} %fusion, bf16[8192,32]{1,0:T(8,128)(2,1)S(1)} %bitcast.39, bf16[128]{0:T(256)(128)(2,1)S(1)} %pad.2.clone), kind=kLoop, calls=%fused_computation.2 | loop fusion | flops 6291456 | bytes 3670272 | tf_op jit(solution)/shard_map/concatenate | solution.py:377
  16.6 0.0 copy-done.4
  16.6 0.1 convert_element_type.31
  16.7 0.0 copy-start.7
  16.7 0.0 copy-start.8
  16.7 0.6 copy.25
  17.3 0.6 copy.18
  17.9 0.0 copy-done.7
  17.9 0.0 copy-start.9
  17.9 0.0 copy-start.1
  17.9 0.0 copy-start.2
  17.9 0.0 copy-start.3
  18.0 0.0 copy-done.8
  18.1 0.1 maximum_bitcast_fusion.g_ref
  18.2 0.4 copy-done.9
  18.6 0.9 copy-done.1
  19.5 0.1 copy-done.2
  19.6 0.0 copy-done.3
  19.6 170.3 %shard_map.136 = bf16[2,128,1024]{2,1,0:T(8,128)(2,1)S(1)} custom-call(bf16[2,128,1024]{2,1,0:T(8,128)(2,1)S(1)} %copy-done.2, s32[2,1,128]{2,1,0:T(1,128)S(1)} %bitcast.38, f32[1,1024]{1,0:T(1,128)S(1)} %convert_element_type.30.gain_ref, bf16[8,64,1280]{2,1,0:T(8,128)(2,1)S(1)} %maximum_bitcast_fusion.g_ref, bf16[64,1280]{1,0:T(8,128)(2,1)S(1)} %pad_maximum_fusion.base_ref, ...), custom_call_target="tpu_custom_call" | custom-call | tf_op jit(solution)/shard_map/pallas_call | solution.py:390
  189.9 0.8 copy.29
  (8 shorter events, 0.1 us)
Async XLA Ops:
  0.0 0.9 copy-start
  1.9 3.9 %copy-start.5 = (bf16[1,8192,64]{1,2,0:T(8,128)(2,1)S(1)}, bf16[1,8192,64]{1,2,0:T(8,128)(2,1)}, u32[]{:S(2)}) copy-start(bf16[1,8192,64]{1,2,0:T(8,128)(2,1)} %param.20) | copy-start | bytes 3145732
  6.8 4.3 %copy-start.6 = (bf16[1,8192,32]{1,2,0:T(8,128)(2,1)S(1)}, bf16[1,8192,32]{1,2,0:T(8,128)(2,1)}, u32[]{:S(2)}) copy-start(bf16[1,8192,32]{1,2,0:T(8,128)(2,1)} %param.18) | copy-start | bytes 1572868
  12.2 4.4 %copy-start.4 = (f32[1,1,64,8192]{3,2,1,0:T(8,128)S(1)}, f32[1,1,64,8192]{3,2,1,0:T(8,128)}, u32[]{:S(2)}) copy-start(f32[1,1,64,8192]{3,2,1,0:T(8,128)} %param.27) | copy-start | bytes 6291460
  16.7 1.2 copy-start.7
  16.7 1.4 copy-start.8
  17.9 0.7 copy-start.9
  17.9 1.6 copy-start.1
  17.9 1.7 copy-start.2
  17.9 1.7 copy-start.3

commit v2 on v1

v2 whole, which is shorter than its diff:
```python
import functools

import jax
import jax.numpy as jnp
from jax import lax
from jax.experimental import pallas as pl
from jax.experimental.pallas import tpu as pltpu
from jax.sharding import PartitionSpec as P

HD = 128
GROUP = 8
RATE = 0.5
EPS = 1e-05
MESH = pl.DeviceIdType.MESH
F32 = jnp.float32
BF16 = jnp.bfloat16


def chain(
    sizes,
    x_ref,
    ends_ref,
    gain_ref,
    bout_ref,
    bq_ref,
    aout_ref,
    gbq_ref,
    gao_ref,
    gbo_hbm,
    aq_hbm,
    gaq_hbm,
    wq_hbm,
    wkv_hbm,
    wo_hbm,
    out_ref,
    wcat,
    side,
    aq,
    gaq,
    gbo,
    merged,
    blocks,
    squares,
    hidden,
    kvx,
    mix,
    aot,
    gout,
    grecv,
    help_in,
    help_out,
    gown,
    gnext,
    bo,
    bpad,
    acc,
    scaled_q,
    w_sem,
    blk_sems,
    sq_sems,
    kv_sems,
    mix_sems,
    ao_sems,
    g_send,
    g_recv,
    hop_send,
    hop_recv,
    in_send,
    in_recv,
    in_on,
    next_send,
    next_recv,
    next_on,
    hid_send,
    hid_recv,
    gain_sem,
):
    n_dp, n_section, kv_cols = sizes
    n = 2 * n_dp
    micro, tok, feat = x_ref.shape
    rank = bout_ref.shape[0]
    width = n * feat
    last = micro - 1
    d, t, s = lax.axis_index("dp"), lax.axis_index("tensor"), lax.axis_index("section")
    me = 2 * d + t

    def along(k):
        return lax.rem(d + k, n_dp)

    def loop(low, high, body):
        def step(k, carry):
            body(k)
            return carry

        lax.fori_loop(low, high, step, jnp.int32(0))

    def remote(src, dst, send, recv, to):
        return pltpu.make_async_remote_copy(
            src_ref=src,
            dst_ref=dst,
            send_sem=send,
            recv_sem=recv,
            device_id=to,
            device_id_type=MESH,
        )

    loads = (
        lambda: pltpu.make_async_copy(wq_hbm, wcat.at[:, pl.ds(0, HD)], w_sem.at[0]),
        lambda: pltpu.make_async_copy(wkv_hbm, side.at[pl.ds(0, kv_cols)], w_sem.at[1]),
        lambda: pltpu.make_async_copy(wo_hbm, merged, w_sem.at[2]),
        lambda: pltpu.make_async_copy(aq_hbm, aq, w_sem.at[3]),
        lambda: pltpu.make_async_copy(gaq_hbm, gaq, w_sem.at[4]),
        lambda: pltpu.make_async_copy(gbo_hbm, gbo, w_sem.at[5]),
    )

    def of(kind, m):
        buffer, (send, on, recv) = (
            (squares, sq_sems),
            (kvx, kv_sems),
            (mix, mix_sems),
            (aot, ao_sems),
            (blocks, blk_sems),
        )[kind]
        return buffer.at[m], send.at[m], on.at[m], recv.at[m]

    def outward(kind, m, k):
        buffer, send, _, recv = of(kind, m)
        return remote(
            buffer.at[me], buffer.at[me], send.at[k], recv.at[me], {"dp": along(k), "tensor": t}
        )

    def sibling(kind, m):
        buffer, send, _, recv = of(kind, m)
        return remote(buffer.at[me], buffer.at[me], send.at[0], recv.at[me], {"tensor": 1 - t})

    def passed(kind, m, k):
        buffer, _, on, recv = of(kind, m)
        i = 2 * along(k) + t
        return remote(buffer.at[i], buffer.at[i], on.at[k], recv.at[i], {"tensor": 1 - t})

    def landed(kind, m, i):
        buffer, send, _, recv = of(kind, m)
        remote(
            buffer.at[i], buffer.at[i], send.at[0], recv.at[i], {"tensor": 1 - t}
        ).wait_recv()

    def share(kind, m):
        loop(1, n_dp, lambda k: outward(kind, m, k).start())
        sibling(kind, m).start()

    def collect(kind, m, use=None):
        def near(k):
            i = 2 * along(k) + t
            landed(kind, m, i)
            passed(kind, m, k).start()
            if use is not None:
                use(i)

        def far(k):
            i = 2 * along(k) + 1 - t
            landed(kind, m, i)
            if use is not None:
                use(i)

        loop(1, n_dp, near)
        loop(0, n_dp, far)

    def sent(kind, m, wide=True):
        if wide:
            loop(1, n_dp, lambda k: outward(kind, m, k).wait_send())
        sibling(kind, m).wait_send()
        loop(1, n_dp, lambda k: passed(kind, m, k).wait_send())

    def grads(k):
        i = along(k)
        to = {"dp": i, "tensor": t}
        return remote(gout.at[2 * i + t], grecv.at[d], g_send.at[k], g_recv.at[d], to)

    def grads_in(k):
        i = along(k)
        to = {"dp": i, "tensor": t}
        return remote(gout.at[me], grecv.at[i], g_send.at[k], g_recv.at[i], to)

    def give_grads():
        loads[5]().wait()

        def fill(j):
            cols = pl.ds(pl.multiple_of(j * feat, feat), feat)
            heads = pl.ds(pl.multiple_of(j * HD, HD), HD)
            gout[j, :, pl.ds(0, feat)] = gbo[:, cols].astype(BF16)
            gout[j, :, pl.ds(feat, HD)] = gbq_ref[:, heads].astype(BF16)
            gout[j, :, pl.ds(feat + HD, HD)] = gao_ref[:, heads].astype(BF16)

        loop(0, n, fill)
        loop(1, n_dp, lambda k: grads(k).start())

    def join_weights():
        for k in (0, 1, 3, 4):
            loads[k]().wait()
        used = kv_cols + rank
        side[pl.ds(used, HD - used), :] = jnp.zeros((HD - used, width), BF16)

        def part(j):
            cols = pl.ds(pl.multiple_of(j * feat, feat), feat)
            own = aq[:, cols].astype(F32) / n_dp - RATE * gaq[:, cols]
            side[pl.ds(kv_cols, rank), cols] = own.astype(BF16)
            wcat[cols, pl.ds(HD, HD)] = jnp.transpose(side[:, cols])

        loop(0, n, part)

    def hop():
        to = {"section": jnp.minimum(s + 1, n_section - 1)}
        return remote(blocks.at[last, me], help_in.at[d], hop_send, hop_recv, to)

    def help_out_copy(buffer, send, recv, k):
        to = {"dp": along(k), "tensor": t}
        return remote(buffer.at[d], buffer.at[d], send.at[k], recv.at[d], to)

    def help_landed(buffer, send, recv, k):
        i = along(k)
        to = {"dp": i, "tensor": t}
        remote(buffer.at[i], buffer.at[i], send.at[k], recv.at[i], to).wait_recv()

    def help_on(buffer, on, k, section):
        i = along(k)
        row = 2 * i + t
        _, _, _, recv = of(4, last)
        return remote(
            buffer.at[i], blocks.at[last, row], on.at[k], recv.at[row], {"section": section}
        )

    before = jnp.maximum(s - 1, 0)
    after = jnp.minimum(s + 1, n_section - 1)

    def gain_copy():
        return remote(gown, gnext, gain_sem.at[0], gain_sem.at[1], {"section": before})

    def gain_landed():
        remote(gown, gnext, gain_sem.at[0], gain_sem.at[1], {"section": after}).wait_recv()

    def onward(m, to):
        return remote(out_ref.at[m], hidden.at[m], hid_send.at[m], hid_recv.at[m], {"section": to})

    def enter(m):
        wide = hidden[m].astype(F32)
        blocks[m, me] = (wide * gain_ref[...]).astype(BF16)
        if m < last:
            share(4, m)
        else:

            @pl.when(s == 0)
            def _():
                hop().start()

            sibling(4, m).start()
        column = jnp.sum(wide * wide, axis=1, keepdims=True)
        squares[m, me] = jnp.transpose(jnp.broadcast_to(column, (tok, HD)))[:8]
        share(0, m)

    def enter_first(m):
        hidden[m] = x_ref[m]
        enter(m)

    def enter_later(m):
        onward(m, before).wait_recv()
        enter(m)

    def project(m):
        def block(i):
            rows = pl.ds(pl.multiple_of(i * feat, feat), feat)
            acc[...] += jnp.dot(blocks[m, i], wcat[rows, :], preferred_element_type=F32)

        acc[...] = jnp.zeros_like(acc)
        block(me)
        collect(4, m, block)
        collect(0, m)
        total = jnp.sum(squares[m], axis=0)[:1]
        column = jnp.transpose(jnp.broadcast_to(total, (tok, HD)))
        inverse = lax.rsqrt(column / width + EPS)
        kvx[m, me] = (acc[:, HD:] * inverse).astype(BF16)
        share(1, m)
        scaled_q[...] = acc[:, :HD] * inverse

    def update():
        total = gout[me].astype(F32)
        loop(1, n_dp, lambda k: grads_in(k).wait_recv())
        for k in range(1, n_dp):
            total = total + grecv[along(k)].astype(F32)
        heads = pl.ds(pl.multiple_of(me * HD, HD), HD)
        total = RATE * total
        fresh = aout_ref[:, heads].astype(F32) - total[:, feat + HD :]
        aot[0, me] = fresh.astype(BF16)
        share(3, 0)
        bo[...] = (bout_ref[...].astype(F32) - total[:, :feat]).astype(BF16)
        fresh = bq_ref[...].astype(F32) - total[:, feat : feat + HD]
        bpad[...] = jnp.zeros_like(bpad)
        bpad[pl.ds(kv_cols, rank), :] = fresh.astype(BF16)

    def merge():
        loads[2]().wait()
        collect(3, 0)

        def rows_of(j):
            rows = pl.ds(pl.multiple_of(j * HD, HD), HD)
            product = lax.dot_general(
                aot[0, j], bo[...], (((0,), (0,)), ((), ())), preferred_element_type=F32
            )
            merged[rows, :] = (merged[rows, :].astype(F32) + product).astype(BF16)

        loop(0, n, rows_of)

    def attend(m):
        collect(1, m)
        query = scaled_q[...]
        for k in range(n_dp):
            query = query + jnp.dot(kvx[m, 2 * k + t], bpad[...], preferred_element_type=F32)
        query = query.astype(BF16)
        per = HD // kv_cols
        first = me // GROUP * 2 * per
        spot = lax.broadcasted_iota(jnp.int32, (HD, HD), 0)
        lane = lax.broadcasted_iota(jnp.int32, (HD, HD), 1)
        keys = jnp.zeros((tok, HD), F32)
        values = jnp.zeros((tok, HD), F32)
        for i in range(per):
            pick = jnp.where((spot < kv_cols) & (lane == spot + i * kv_cols), 1.0, 0.0).astype(BF16)
            keys = keys + jnp.dot(kvx[m, first + i], pick, preferred_element_type=F32)
            values = values + jnp.dot(kvx[m, first + per + i], pick, preferred_element_type=F32)
        scores = lax.dot_general(
            query, keys.astype(BF16), (((1,), (1,)), ((), ())), preferred_element_type=F32
        ) * HD ** (-0.5)
        here = lax.broadcasted_iota(jnp.int32, (tok, tok), 0)
        there = lax.broadcasted_iota(jnp.int32, (tok, tok), 1)
        visible = (there <= here) & (ends_ref[m] >= here)
        scores = jnp.where(visible, scores, -1e30)
        raised = jnp.exp(scores - jnp.max(scores, axis=-1, keepdims=True))
        portion = (raised / jnp.sum(raised, axis=-1, keepdims=True)).astype(BF16)
        mixed = jnp.dot(portion, values.astype(BF16), preferred_element_type=F32)
        mix[m, me] = mixed.astype(BF16)
        share(2, m)

    def leave(m):
        collect(2, m)
        heads = jnp.concatenate([mix[m, j] for j in range(n)], axis=1)
        total = jnp.dot(heads, merged[...], preferred_element_type=F32)
        out_ref[m] = (hidden[m].astype(F32) + total).astype(BF16)

        @pl.when(s < n_section - 1)
        def _():
            onward(m, after).start()
            if m == last:
                gain_landed()
                help_out[d] = (out_ref[m].astype(F32) * gnext[:1]).astype(BF16)
                loop(1, n_dp, lambda k: help_out_copy(help_out, next_send, next_recv, k).start())

                def relay(k):
                    help_landed(help_out, next_send, next_recv, k)
                    help_on(help_out, next_on, k, after).start()

                loop(1, n_dp, relay)

    for load in loads:
        load().start()
    gown[...] = jnp.broadcast_to(gain_ref[...], gown.shape)
    barrier = pltpu.get_barrier_semaphore()

    def greet(k):
        i = lax.rem(me + k, n)
        to = {"dp": i // 2, "tensor": lax.rem(i, 2)}
        pl.semaphore_signal(barrier, inc=1, device_id=to, device_id_type=MESH)

    loop(1, n, greet)

    @pl.when(s > 0)
    def _():
        pl.semaphore_signal(barrier, inc=1, device_id={"section": s - 1}, device_id_type=MESH)

    @pl.when(s < n_section - 1)
    def _():
        pl.semaphore_signal(barrier, inc=1, device_id={"section": s + 1}, device_id_type=MESH)

    sections = (s > 0).astype(jnp.int32) + (s < n_section - 1).astype(jnp.int32)
    pl.semaphore_wait(barrier, n - 1 + sections)

    @pl.when(s == 0)
    def _():
        for m in range(micro):
            enter_first(m)

    @pl.when(s > 0)
    def _():
        gain_copy().start()

    give_grads()

    @pl.when(s == 1)
    def _():
        remote(blocks.at[last, me], help_in.at[d], hop_send, hop_recv, {"section": 0}).wait_recv()
        loop(1, n_dp, lambda k: help_out_copy(help_in, in_send, in_recv, k).start())

    join_weights()

    @pl.when(s == 1)
    def _():
        def relay(k):
            help_landed(help_in, in_send, in_recv, k)
            help_on(help_in, in_on, k, 0).start()

        loop(1, n_dp, relay)

    @pl.when(s > 0)
    def _():
        update()
        merge()
        enter_later(0)

    for m in range(micro):
        project(m)
        if m == 0:

            @pl.when(s == 0)
            def _():
                update()

        if m + 1 < micro:

            @pl.when(s > 0)
            def _(m=m):
                enter_later(m + 1)

        attend(m)
        if m == 0:

            @pl.when(s == 0)
            def _():
                merge()

        leave(m)

    loop(1, n_dp, lambda k: grads(k).wait_send())
    sent(3, 0)
    for m in range(micro):
        for kind in range(3):
            sent(kind, m)
        sent(4, m, m < last)

    @pl.when(s == 0)
    def _():
        hop().wait_send()

    @pl.when(s == 1)
    def _():
        loop(1, n_dp, lambda k: help_out_copy(help_in, in_send, in_recv, k).wait_send())
        loop(1, n_dp, lambda k: help_on(help_in, in_on, k, 0).wait_send())

    @pl.when(s > 0)
    def _():
        gain_copy().wait_send()

    @pl.when(s < n_section - 1)
    def _():
        for m in range(micro):
            onward(m, after).wait_send()
        loop(1, n_dp, lambda k: help_out_copy(help_out, next_send, next_recv, k).wait_send())
        loop(1, n_dp, lambda k: help_on(help_out, next_on, k, after).wait_send())


def on_device(
    x_in,
    subtree_end,
    norm_gain,
    w_query,
    w_kv,
    w_out,
    a_query,
    b_query,
    a_out,
    b_out,
    grad_a_query,
    grad_b_query,
    grad_a_out,
    grad_b_out,
):
    n_dp, n_section = lax.axis_size("dp"), lax.axis_size("section")
    n = 2 * n_dp
    micro, tok, feat = x_in.shape
    width, kv_cols = w_kv.shape[1:]
    rank = a_query.shape[2]
    vmem = pl.BlockSpec(memory_space=pltpu.VMEM)
    hbm = pl.BlockSpec(memory_space=pl.ANY)
    dma = pltpu.SemaphoreType.DMA
    extra = feat + 2 * HD

    def exchange(count):
        return (dma((count, n_dp)), dma((count, n_dp)), dma((count, n)))

    return pl.pallas_call(
        functools.partial(chain, (n_dp, n_section, kv_cols)),
        out_shape=jax.ShapeDtypeStruct((micro, tok, feat), BF16),
        in_specs=[vmem] * 8 + [hbm] * 6,
        out_specs=vmem,
        scratch_shapes=[
            pltpu.VMEM((width, 2 * HD), BF16),
            pltpu.VMEM((HD, width), BF16),
            pltpu.VMEM((rank, width), BF16),
            pltpu.VMEM((rank, width), F32),
            pltpu.VMEM((rank, width), F32),
            pltpu.VMEM((n * HD, feat), BF16),
            pltpu.VMEM((micro, n, tok, feat), BF16),
            pltpu.VMEM((micro, n, 8, HD), F32),
            pltpu.VMEM((micro, tok, feat), BF16),
            pltpu.VMEM((micro, n, tok, HD), BF16),
            pltpu.VMEM((micro, n, tok, HD), BF16),
            pltpu.VMEM((1, n, rank, HD), BF16),
            pltpu.VMEM((n, rank, extra), BF16),
            pltpu.VMEM((n_dp, rank, extra), BF16),
            pltpu.VMEM((n_dp, tok, feat), BF16),
            pltpu.VMEM((n_dp, tok, feat), BF16),
            pltpu.VMEM((8, feat), F32),
            pltpu.VMEM((8, feat), F32),
            pltpu.VMEM((rank, feat), BF16),
            pltpu.VMEM((HD, HD), BF16),
            pltpu.VMEM((tok, 2 * HD), F32),
            pltpu.VMEM((tok, HD), F32),
            dma((6,)),
            exchange(micro),
            exchange(micro),
            exchange(micro),
            exchange(micro),
            exchange(1),
            dma((n_dp,)),
            dma((n_dp,)),
            dma,
            dma,
            dma((n_dp,)),
            dma((n_dp,)),
            dma((n_dp,)),
            dma((n_dp,)),
            dma((n_dp,)),
            dma((n_dp,)),
            dma((micro,)),
            dma((micro,)),
            dma((2,)),
        ],
        compiler_params=pltpu.CompilerParams(
            collective_id=0, has_side_effects=True, vmem_limit_bytes=48 * 2**20
        ),
    )(
        x_in,
        subtree_end[:, None, :],
        norm_gain.astype(F32),
        b_out[0],
        b_query[0],
        a_out[0].T,
        grad_b_query[0, 0],
        grad_a_out[0, 0].T,
        grad_b_out[0, 0],
        a_query[0].T,
        grad_a_query[0, 0].T,
        w_query[0],
        w_kv[0].T,
        w_out[0],
    )[None]


def solution(mesh):
    placed = (
        P("groups", None, ("dp", "tensor")),
        P("groups", None),
        P("section", ("dp", "tensor")),
        P("section", None, ("dp", "tensor")),
        P("section", None, ("dp", "tensor")),
        P("section", None, ("dp", "tensor")),
        P("section", None, None),
        P("section", None, ("dp", "tensor")),
        P("section", None, None),
        P("section", None, ("dp", "tensor")),
        P("section", "dp", None, None),
        P("section", "dp", None, None),
        P("section", "dp", None, None),
        P("section", "dp", None, None),
    )
    return jax.shard_map(
        on_device,
        mesh=mesh,
        in_specs=placed,
        out_specs=P("section", "groups", None, ("dp", "tensor")),
        check_vma=False,
    )
```

time: 191 us -> 143 us (0.75)
  Pallas kernels: 170 us -> 131 us
  other arithmetic: 9.81 us -> 0.69 us
    pallas_call x1, Pallas kernels: 170 us -> 131 us  [on_device(): pl.pallas_call(functools.partial(chain, (n_dp, n_section, kv_cols)), out_...]
    concatenate x2 -> x0, other arithmetic: 5.3 us -> none  [the longest x1 4.36 us: on_device(): w_side = jnp.concatenate([w_kv[0], own, rest], axis=1)]
    convert_element_type x2 -> x0, other arithmetic: 4.35 us -> none  [the longest x1 4.24 us: on_device(): (a_query[0].astype(F32) / n_dp - RATE * grad_a_query[0, 0]).astype(BF16)]
    unnamed x26 -> x21, local copies, waits for them, and re-layouts: 9.72 us -> 10.8 us
where the time goes in v2:
time: 143 us
  Pallas kernels  131 us (92%)
  local copies, waits for them, and re-layouts  10.8 us (8%)
    pallas_call x1, Pallas kernels, on_device(): pl.pallas_call(functools.partial(chain, (n_dp, n_section, kv_cols)), out_...  131 us
    unnamed x21, local copies, waits for them, and re-layouts  10.8 us

profile of v2, /device:TPU:3, one launch (start us, length us, event | category | flops | bytes accessed | tf_op | source)
XLA Modules:
  0.0 142.5 jit_solution(12213131214471997636)
XLA Ops:
  0.0 0.7 convert_element_type.3.gain_ref
  0.7 0.0 copy-start
  0.7 1.6 %copy-done = f32[1,1,64,8192]{3,2,1,0:T(8,128)S(1)} copy-done((f32[1,1,64,8192]{3,2,1,0:T(8,128)S(1)}, f32[1,1,64,8192]{3,2,1,0:T(8,128)}, u32[]{:S(2)}) %copy-start) | copy-done | bytes 2097176
  2.3 0.0 copy-start.1
  2.3 1.2 copy-done.1
  3.5 0.0 copy-start.2
  3.5 1.0 copy-done.2
  4.6 0.0 copy-start.3
  4.6 1.0 copy-done.3
  5.6 0.0 copy-start.4
  5.6 0.9 copy-done.4
  6.5 0.0 copy-start.5
  6.5 0.9 copy-done.5
  7.5 0.0 copy-start.6
  7.5 0.9 copy-done.6
  8.4 0.0 copy-start.7
  8.4 0.9 copy-done.7
  9.3 0.0 copy-start.8
  9.3 0.7 copy-done.8
  10.0 0.0 copy-start.9
  10.0 0.7 copy-done.9
  10.7 131.0 %shard_map.136 = bf16[2,128,1024]{2,1,0:T(8,128)(2,1)S(1)} custom-call(bf16[2,128,1024]{2,1,0:T(8,128)(2,1)S(1)} %copy-done.2, s32[2,1,128]{2,1,0:T(1,128)S(1)} %bitcast.32, f32[1,1024]{1,0:T(1,128)S(1)} %convert_element_type.3.gain_ref, bf16[64,1024]{1,0:T(8,128)(2,1)S(1)} %bitcast.29, bf16[64,128]{1,0:T(8,128)(2,1)S(1)} %bitcast.31, ...), custom_call_target="tpu_custom_call" | custom-call | tf_op jit(solution)/shard_map/pallas_call | solution.py:496
  141.7 0.8 copy.16
Async XLA Ops:
  0.7 1.6 %copy-start = (f32[1,1,64,8192]{3,2,1,0:T(8,128)S(1)}, f32[1,1,64,8192]{3,2,1,0:T(8,128)}, u32[]{:S(2)}) copy-start(f32[1,1,64,8192]{3,2,1,0:T(8,128)} %param.27) | copy-start | bytes 6291460
  2.3 1.2 copy-start.1
  3.5 1.0 copy-start.2
  4.6 1.0 copy-start.3
  5.6 0.9 copy-start.4
  6.5 0.9 copy-start.5
  7.5 0.9 copy-start.6
  8.4 0.9 copy-start.7
  9.3 0.7 copy-start.8
  10.0 0.7 copy-start.9

commit v3 on v2

--- a/solution.py
+++ b/solution.py
@@ -18,14 +18,14 @@
 
 def chain(
     sizes,
-    x_ref,
     ends_ref,
     gain_ref,
-    bout_ref,
-    bq_ref,
-    aout_ref,
-    gbq_ref,
-    gao_ref,
+    x_hbm,
+    bout_hbm,
+    bq_hbm,
+    aout_hbm,
+    gbq_hbm,
+    gao_hbm,
     gbo_hbm,
     aq_hbm,
     gaq_hbm,
@@ -38,6 +38,11 @@
     aq,
     gaq,
     gbo,
+    bout_ref,
+    bq_ref,
+    aout_ref,
+    gbq_ref,
+    gao_ref,
     merged,
     blocks,
     squares,
@@ -47,6 +52,7 @@
     aot,
     gout,
     grecv,
+    halves,
     help_in,
     help_out,
     gown,
@@ -74,15 +80,22 @@
     hid_send,
     hid_recv,
     gain_sem,
+    half_recv,
+    low_send,
+    y_sem,
+    x_sem,
 ):
     n_dp, n_section, kv_cols = sizes
     n = 2 * n_dp
-    micro, tok, feat = x_ref.shape
+    micro, tok, feat = hidden.shape
     rank = bout_ref.shape[0]
     width = n * feat
     last = micro - 1
     d, t, s = lax.axis_index("dp"), lax.axis_index("tensor"), lax.axis_index("section")
+    y = lax.axis_index("groups")
     me = 2 * d + t
+    cut = tok // 2
+    half = rank // 2
 
     def along(k):
         return lax.rem(d + k, n_dp)
@@ -111,6 +124,11 @@
         lambda: pltpu.make_async_copy(aq_hbm, aq, w_sem.at[3]),
         lambda: pltpu.make_async_copy(gaq_hbm, gaq, w_sem.at[4]),
         lambda: pltpu.make_async_copy(gbo_hbm, gbo, w_sem.at[5]),
+        lambda: pltpu.make_async_copy(gbq_hbm, gbq_ref, w_sem.at[6]),
+        lambda: pltpu.make_async_copy(gao_hbm, gao_ref, w_sem.at[7]),
+        lambda: pltpu.make_async_copy(bout_hbm, bout_ref, w_sem.at[8]),
+        lambda: pltpu.make_async_copy(bq_hbm, bq_ref, w_sem.at[9]),
+        lambda: pltpu.make_async_copy(aout_hbm, aout_ref, w_sem.at[10]),
     )
 
     def of(kind, m):
@@ -151,7 +169,13 @@
     def collect(kind, m, use=None):
         def near(k):
             i = 2 * along(k) + t
-            landed(kind, m, i)
+            if kind == 4 and m == last:
+                for part in range(2):
+                    rows = blocks.at[m, i, pl.ds(part * cut, cut)]
+                    sem = half_recv.at[part, i]
+                    remote(rows, rows, low_send.at[k], sem, {"tensor": 1 - t}).wait_recv()
+            else:
+                landed(kind, m, i)
             passed(kind, m, k).start()
             if use is not None:
                 use(i)
@@ -174,15 +198,23 @@
     def grads(k):
         i = along(k)
         to = {"dp": i, "tensor": t}
-        return remote(gout.at[2 * i + t], grecv.at[d], g_send.at[k], g_recv.at[d], to)
+        rows = pl.ds(pl.multiple_of(y * half, half), half)
+        return remote(
+            gout.at[2 * i + t, rows], grecv.at[d, rows], g_send.at[k], g_recv.at[d], to
+        )
 
     def grads_in(k):
         i = along(k)
         to = {"dp": i, "tensor": t}
-        return remote(gout.at[me], grecv.at[i], g_send.at[k], g_recv.at[i], to)
+        rows = pl.ds(pl.multiple_of(y * half, half), half)
+        return remote(gout.at[me, rows], grecv.at[i, rows], g_send.at[k], g_recv.at[i], to)
+
+    def sums(k):
+        return remote(halves.at[k], halves.at[k], y_sem.at[0], y_sem.at[1 + k], {"groups": 1 - y})
 
     def give_grads():
-        loads[5]().wait()
+        for k in (5, 6, 7):
+            loads[k]().wait()
 
         def fill(j):
             cols = pl.ds(pl.multiple_of(j * feat, feat), feat)
@@ -212,22 +244,33 @@
         to = {"section": jnp.minimum(s + 1, n_section - 1)}
         return remote(blocks.at[last, me], help_in.at[d], hop_send, hop_recv, to)
 
-    def help_out_copy(buffer, send, recv, k):
+    def help_copy(buffer, send, recv, k, part):
         to = {"dp": along(k), "tensor": t}
-        return remote(buffer.at[d], buffer.at[d], send.at[k], recv.at[d], to)
-
-    def help_landed(buffer, send, recv, k):
+        rows = buffer.at[d, pl.ds(part * cut, cut)]
+        return remote(rows, rows, send.at[part, k], recv.at[part, d], to)
+
+    def help_landed(buffer, send, recv, k, part):
         i = along(k)
         to = {"dp": i, "tensor": t}
-        remote(buffer.at[i], buffer.at[i], send.at[k], recv.at[i], to).wait_recv()
-
-    def help_on(buffer, on, k, section):
+        rows = buffer.at[i, pl.ds(part * cut, cut)]
+        remote(rows, rows, send.at[part, k], recv.at[part, i], to).wait_recv()
+
+    def help_on(buffer, on, k, part, section):
         i = along(k)
         row = 2 * i + t
-        _, _, _, recv = of(4, last)
+        rows = pl.ds(part * cut, cut)
         return remote(
-            buffer.at[i], blocks.at[last, row], on.at[k], recv.at[row], {"section": section}
+            buffer.at[i, rows],
+            blocks.at[last, row, rows],
+            on.at[part, k],
+            half_recv.at[part, row],
+            {"section": section},
         )
+
+    def lower(k):
+        rows = blocks.at[last, me, pl.ds(cut, cut)]
+        to = {"dp": along(k), "tensor": t}
+        return remote(rows, rows, low_send.at[k], half_recv.at[1, me], to)
 
     before = jnp.maximum(s - 1, 0)
     after = jnp.minimum(s + 1, n_section - 1)
@@ -243,7 +286,7 @@
 
     def enter(m):
         wide = hidden[m].astype(F32)
-        blocks[m, me] = (wide * gain_ref[...]).astype(BF16)
+        blocks[m, me] = (wide * gown[:1]).astype(BF16)
         if m < last:
             share(4, m)
         else:
@@ -251,14 +294,21 @@
             @pl.when(s == 0)
             def _():
                 hop().start()
+
+            @pl.when(s > 0)
+            def _():
+                loop(1, n_dp, lambda k: lower(k).start())
 
             sibling(4, m).start()
         column = jnp.sum(wide * wide, axis=1, keepdims=True)
         squares[m, me] = jnp.transpose(jnp.broadcast_to(column, (tok, HD)))[:8]
         share(0, m)
 
+    def entering(m):
+        return pltpu.make_async_copy(x_hbm.at[m], hidden.at[m], x_sem.at[m])
+
     def enter_first(m):
-        hidden[m] = x_ref[m]
+        entering(m).wait()
         enter(m)
 
     def enter_later(m):
@@ -282,10 +332,17 @@
         scaled_q[...] = acc[:, :HD] * inverse
 
     def update():
-        total = gout[me].astype(F32)
+        rows = pl.ds(pl.multiple_of(y * half, half), half)
+        total = gout[me, rows].astype(F32)
         loop(1, n_dp, lambda k: grads_in(k).wait_recv())
         for k in range(1, n_dp):
-            total = total + grecv[along(k)].astype(F32)
+            total = total + grecv[along(k), rows].astype(F32)
+        halves[y] = total.astype(BF16)
+        sums(y).start()
+        for k in (8, 9, 10):
+            loads[k]().wait()
+        sums(1 - y).wait_recv()
+        total = jnp.concatenate([halves[0], halves[1]], axis=0).astype(F32)
         heads = pl.ds(pl.multiple_of(me * HD, HD), HD)
         total = RATE * total
         fresh = aout_ref[:, heads].astype(F32) - total[:, feat + HD :]
@@ -349,18 +406,24 @@
             onward(m, after).start()
             if m == last:
                 gain_landed()
-                help_out[d] = (out_ref[m].astype(F32) * gnext[:1]).astype(BF16)
-                loop(1, n_dp, lambda k: help_out_copy(help_out, next_send, next_recv, k).start())
+                upper = out_ref[m, pl.ds(0, cut), :].astype(F32)
+                help_out[d, pl.ds(0, cut), :] = (upper * gnext[:1]).astype(BF16)
+                loop(1, n_dp, lambda k: help_copy(help_out, next_send, next_recv, k, 0).start())
 
                 def relay(k):
-                    help_landed(help_out, next_send, next_recv, k)
-                    help_on(help_out, next_on, k, after).start()
+                    help_landed(help_out, next_send, next_recv, k, 0)
+                    help_on(help_out, next_on, k, 0, after).start()
 
                 loop(1, n_dp, relay)
 
-    for load in loads:
-        load().start()
-    gown[...] = jnp.broadcast_to(gain_ref[...], gown.shape)
+    @pl.when(s == 0)
+    def _():
+        for m in range(micro):
+            entering(m).start()
+
+    for k in (5, 6, 7, 4, 3, 1, 0, 2, 8, 9, 10):
+        loads[k]().start()
+    gown[...] = jnp.broadcast_to(gain_ref[...].astype(F32), gown.shape)
     barrier = pltpu.get_barrier_semaphore()
 
     def greet(k):
@@ -369,6 +432,7 @@
         pl.semaphore_signal(barrier, inc=1, device_id=to, device_id_type=MESH)
 
     loop(1, n, greet)
+    pl.semaphore_signal(barrier, inc=1, device_id={"groups": 1 - y}, device_id_type=MESH)
 
     @pl.when(s > 0)
     def _():
@@ -379,7 +443,7 @@
         pl.semaphore_signal(barrier, inc=1, device_id={"section": s + 1}, device_id_type=MESH)
 
     sections = (s > 0).astype(jnp.int32) + (s < n_section - 1).astype(jnp.int32)
-    pl.semaphore_wait(barrier, n - 1 + sections)
+    pl.semaphore_wait(barrier, n + sections)
 
     @pl.when(s == 0)
     def _():
@@ -390,28 +454,30 @@
     def _():
         gain_copy().start()
 
+    @pl.when(s == 1)
+    def _():
+        remote(blocks.at[last, me], help_in.at[d], hop_send, hop_recv, {"section": 0}).wait_recv()
+        for part in range(2):
+            loop(1, n_dp, lambda k: help_copy(help_in, in_send, in_recv, k, part).start())
+
     give_grads()
+    join_weights()
 
     @pl.when(s == 1)
     def _():
-        remote(blocks.at[last, me], help_in.at[d], hop_send, hop_recv, {"section": 0}).wait_recv()
-        loop(1, n_dp, lambda k: help_out_copy(help_in, in_send, in_recv, k).start())
-
-    join_weights()
-
-    @pl.when(s == 1)
-    def _():
-        def relay(k):
-            help_landed(help_in, in_send, in_recv, k)
-            help_on(help_in, in_on, k, 0).start()
-
-        loop(1, n_dp, relay)
+        for part in range(2):
+
+            def relay(k):
+                help_landed(help_in, in_send, in_recv, k, part)
+                help_on(help_in, in_on, k, part, 0).start()
+
+            loop(1, n_dp, relay)
 
     @pl.when(s > 0)
     def _():
+        enter_later(0)
         update()
         merge()
-        enter_later(0)
 
     for m in range(micro):
         project(m)
@@ -437,6 +503,7 @@
         leave(m)
 
     loop(1, n_dp, lambda k: grads(k).wait_send())
+    sums(y).wait_send()
     sent(3, 0)
     for m in range(micro):
         for kind in range(3):
@@ -449,19 +516,21 @@
 
     @pl.when(s == 1)
     def _():
-        loop(1, n_dp, lambda k: help_out_copy(help_in, in_send, in_recv, k).wait_send())
-        loop(1, n_dp, lambda k: help_on(help_in, in_on, k, 0).wait_send())
+        for part in range(2):
+            loop(1, n_dp, lambda k: help_copy(help_in, in_send, in_recv, k, part).wait_send())
+            loop(1, n_dp, lambda k: help_on(help_in, in_on, k, part, 0).wait_send())
 
     @pl.when(s > 0)
     def _():
         gain_copy().wait_send()
+        loop(1, n_dp, lambda k: lower(k).wait_send())
 
     @pl.when(s < n_section - 1)
     def _():
         for m in range(micro):
             onward(m, after).wait_send()
-        loop(1, n_dp, lambda k: help_out_copy(help_out, next_send, next_recv, k).wait_send())
-        loop(1, n_dp, lambda k: help_on(help_out, next_on, k, after).wait_send())
+        loop(1, n_dp, lambda k: help_copy(help_out, next_send, next_recv, k, 0).wait_send())
+        loop(1, n_dp, lambda k: help_on(help_out, next_on, k, 0, after).wait_send())
 
 
 def on_device(
@@ -486,7 +555,7 @@
     width, kv_cols = w_kv.shape[1:]
     rank = a_query.shape[2]
     vmem = pl.BlockSpec(memory_space=pltpu.VMEM)
-    hbm = pl.BlockSpec(memory_space=pl.ANY)
+    hbm = pl.BlockSpec(memory_space=pltpu.HBM)
     dma = pltpu.SemaphoreType.DMA
     extra = feat + 2 * HD
 
@@ -496,7 +565,7 @@
     return pl.pallas_call(
         functools.partial(chain, (n_dp, n_section, kv_cols)),
         out_shape=jax.ShapeDtypeStruct((micro, tok, feat), BF16),
-        in_specs=[vmem] * 8 + [hbm] * 6,
+        in_specs=[vmem] * 2 + [hbm] * 12,
         out_specs=vmem,
         scratch_shapes=[
             pltpu.VMEM((width, 2 * HD), BF16),
@@ -504,6 +573,11 @@
             pltpu.VMEM((rank, width), BF16),
             pltpu.VMEM((rank, width), F32),
             pltpu.VMEM((rank, width), F32),
+            pltpu.VMEM((rank, feat), BF16),
+            pltpu.VMEM((rank, HD), BF16),
+            pltpu.VMEM((rank, n * HD), BF16),
+            pltpu.VMEM((rank, n * HD), F32),
+            pltpu.VMEM((rank, n * HD), F32),
             pltpu.VMEM((n * HD, feat), BF16),
             pltpu.VMEM((micro, n, tok, feat), BF16),
             pltpu.VMEM((micro, n, 8, HD), F32),
@@ -513,6 +587,7 @@
             pltpu.VMEM((1, n, rank, HD), BF16),
             pltpu.VMEM((n, rank, extra), BF16),
             pltpu.VMEM((n_dp, rank, extra), BF16),
+            pltpu.VMEM((2, rank // 2, extra), BF16),
             pltpu.VMEM((n_dp, tok, feat), BF16),
             pltpu.VMEM((n_dp, tok, feat), BF16),
             pltpu.VMEM((8, feat), F32),
@@ -521,7 +596,7 @@
             pltpu.VMEM((HD, HD), BF16),
             pltpu.VMEM((tok, 2 * HD), F32),
             pltpu.VMEM((tok, HD), F32),
-            dma((6,)),
+            dma((11,)),
             exchange(micro),
             exchange(micro),
             exchange(micro),
@@ -531,23 +606,27 @@
             dma((n_dp,)),
             dma,
             dma,
-            dma((n_dp,)),
-            dma((n_dp,)),
-            dma((n_dp,)),
-            dma((n_dp,)),
-            dma((n_dp,)),
-            dma((n_dp,)),
+            dma((2, n_dp)),
+            dma((2, n_dp)),
+            dma((2, n_dp)),
+            dma((2, n_dp)),
+            dma((2, n_dp)),
+            dma((2, n_dp)),
             dma((micro,)),
             dma((micro,)),
             dma((2,)),
+            dma((2, n)),
+            dma((n_dp,)),
+            dma((3,)),
+            dma((micro,)),
         ],
         compiler_params=pltpu.CompilerParams(
             collective_id=0, has_side_effects=True, vmem_limit_bytes=48 * 2**20
         ),
     )(
+        subtree_end[:, None, :],
+        norm_gain,
         x_in,
-        subtree_end[:, None, :],
-        norm_gain.astype(F32),
         b_out[0],
         b_query[0],
         a_out[0].T,

time: 143 us -> 140 us (0.979); the launches traced: 143 us -> 137 us
  Pallas kernels: 131 us -> 126 us
    pallas_call x1, Pallas kernels: 131 us -> 126 us  [on_device(): pl.pallas_call(functools.partial(chain, (n_dp, n_section, kv_cols)), out_...]
    unnamed x21 -> x23, local copies, waits for them, and re-layouts: 10.8 us -> 11.5 us
where the time goes in v3:
time: 140 us; the launch traced here: 137 us
  Pallas kernels  126 us (90%)
  local copies, waits for them, and re-layouts  11.5 us (8%)
    pallas_call x1, Pallas kernels, on_device(): pl.pallas_call(functools.partial(chain, (n_dp, n_section, kv_cols)), out_...  126 us
    unnamed x23, local copies, waits for them, and re-layouts  11.5 us

profile of v3, /device:TPU:3, one launch (start us, length us, event | category | flops | bytes accessed | tf_op | source)
XLA Modules:
  0.0 137.3 jit_solution(17545060975132842629)
XLA Ops:
  0.0 0.0 copy-start
  0.0 1.6 %copy-done = f32[1,1,64,8192]{3,2,1,0:T(8,128)S(1)} copy-done((f32[1,1,64,8192]{3,2,1,0:T(8,128)S(1)}, f32[1,1,64,8192]{3,2,1,0:T(8,128)}, u32[]{:S(2)}) %copy-start) | copy-done | bytes 2097176
  1.6 0.0 copy-start.1
  1.6 1.2 copy-done.1
  2.8 0.0 copy-start.2
  2.8 1.0 copy-done.2
  3.9 0.0 copy-start.3
  3.9 1.0 copy-done.3
  4.9 0.0 copy-start.4
  4.9 0.9 copy-done.4
  5.9 0.0 copy-start.5
  5.9 0.9 copy-done.5
  6.8 0.0 copy-start.6
  6.8 0.9 copy-done.6
  7.7 0.0 copy-start.7
  7.7 0.9 copy-done.7
  8.6 0.0 copy-start.8
  8.6 0.7 copy-done.8
  9.3 0.0 copy-start.9
  9.3 0.7 copy-done.9
  10.0 0.0 copy-start.10
  10.0 0.7 copy-done.10
  10.7 125.8 %shard_map.136 = bf16[2,128,1024]{2,1,0:T(8,128)(2,1)S(1)} custom-call(s32[2,1,128]{2,1,0:T(1,128)S(1)} %bitcast.32, bf16[1,1024]{1,0:T(2,128)(2,1)S(1)} %copy-done.9, bf16[2,128,1024]{2,1,0:T(8,128)(2,1)S(1)} %copy-done.2, bf16[64,1024]{1,0:T(8,128)(2,1)S(1)} %bitcast.29, bf16[64,128]{1,0:T(8,128)(2,1)S(1)} %bitcast.31, bf16[64,1024]{1,0:T(8,128)(2,1)S(1)} %bitcast.30, ...), custom_call_target="tpu_custom_call" | custom-call | tf_op jit(solution)/shard_map/pallas_call | solution.py:565
  136.5 0.8 copy.16
Async XLA Ops:
  0.0 1.6 %copy-start = (f32[1,1,64,8192]{3,2,1,0:T(8,128)S(1)}, f32[1,1,64,8192]{3,2,1,0:T(8,128)}, u32[]{:S(2)}) copy-start(f32[1,1,64,8192]{3,2,1,0:T(8,128)} %param.27) | copy-start | bytes 6291460
  1.6 1.2 copy-start.1
  2.8 1.0 copy-start.2
  3.9 1.0 copy-start.3
  4.9 0.9 copy-start.4
  5.9 0.9 copy-start.5
  6.8 0.9 copy-start.6
  7.7 0.9 copy-start.7
  8.6 0.7 copy-start.8
  9.3 0.7 copy-start.9
  10.0 0.7 copy-start.10

commit v4 on v3

--- a/solution.py
+++ b/solution.py
@@ -621,7 +621,7 @@
             dma((micro,)),
         ],
         compiler_params=pltpu.CompilerParams(
-            collective_id=0, has_side_effects=True, vmem_limit_bytes=48 * 2**20
+            collective_id=0, has_side_effects=True, vmem_limit_bytes=63 * 2**20
         ),
     )(
         subtree_end[:, None, :],

time: 140 us -> 133 us (0.950); the launches traced: 137 us -> 133 us
  local copies, waits for them, and re-layouts: 11.5 us -> 1.87 us
  Pallas kernels: 126 us -> 131 us
    unnamed x23 -> x1, local copies, waits for them, and re-layouts: 11.5 us -> 1.87 us
    pallas_call x1, Pallas kernels: 126 us -> 131 us  [on_device(): pl.pallas_call(functools.partial(chain, (n_dp, n_section, kv_cols)), out_...]
where the time goes in v4:
time: 133 us
  Pallas kernels  131 us (98%)
  local copies, waits for them, and re-layouts  1.87 us (1%)
    pallas_call x1, Pallas kernels, on_device(): pl.pallas_call(functools.partial(chain, (n_dp, n_section, kv_cols)), out_...  131 us

profile of v4, /device:TPU:3, one launch (start us, length us, event | category | flops | bytes accessed | tf_op | source)
XLA Modules:
  0.0 132.6 jit_solution(10988345940403965946)
XLA Ops:
  0.0 130.7 %shard_map.136 = bf16[2,128,1024]{2,1,0:T(8,128)(2,1)} custom-call(s32[2,1,128]{2,1,0:T(1,128)} %bitcast.35, bf16[1,1024]{1,0:T(2,128)(2,1)} %gain_ref.1, bf16[2,128,1024]{2,1,0:T(8,128)(2,1)} %x_hbm.1, bf16[64,1024]{1,0:T(8,128)(2,1)} %bitcast.32, bf16[64,128]{1,0:T(8,128)(2,1)} %bitcast.34, bf16[64,1024]{1,0:T(8,128)(2,1)} %bitcast.33, ...), custom_call_target="tpu_custom_call" | custom-call | tf_op jit(solution)/shard_map/pallas_call | solution.py:565
  130.7 1.9 %copy.16 = bf16[1,2,128,1024]{3,2,1,0:T(8,128)(2,1)} copy(bf16[1,2,128,1024]{3,2,1,0:T(8,128)(2,1)} %bitcast.23) | data formatting | bytes 1048576
